TPU v7x, 128 devices: a whole 4x4x4 slice. The times are simulated.
128 devices in a mesh: shot: 16 (over y, x_hi, core), pt: 8 (over z, x_lo).
Axes of the slice: x: 4 (x_hi: 2, x_lo: 2; x = x_hi * 2 + x_lo), y: 4, z: 4, core: 2. Of those that a mesh axis runs over, the one named last changes fastest.
Arguments:
- shot_data: bfloat16 [256, 128, 1024], P('shot', 'pt'), may hold values from -0.29882812 to 0.29882812
- point_store: bfloat16 [128, 576, 1024], P(('shot', 'pt')), may hold values from -0.29882812 to 0.29882812
- point_slot: int32 [128], P('pt'), may hold values from 0 to 127, as said below
- taper_mask: int32 [256, 128], P('shot', 'pt'), may hold values 0 or 1
- recv_start: int32 [256], P('shot'), may hold values from 0 to 64
Outputs:
- multiples: float32 [256, 512, 1024], P('shot', 'pt')
Inputs may be any that keep to these rules, and one draw needn't show every extreme that they name: `point_slot`: A permutation of the slots; the gathers of the inner points k with k // 16 = b lie in the slots q with (q) % (8) = b.
All inputs are finite; a program needn't handle non-finite values. No bound on the sum of `taper_mask` on one device may be relied on, other than what follows from the above.
Results may differ from a plain program's by a relative error of at most 0.0063.
Values may be sent and summed in bfloat16 or wider, within the bound.
No kernel may reach another device: no remote copies, remote signals or barrier semaphores. Data moves between devices by JAX's collectives and lax.ppermute only.
A program may use at most 192 MiB of HBM per device.

v0:
```python
import functools
import math

import jax
import jax.numpy as jnp
import numpy as np
from jax import lax
from jax.experimental import pallas as pl
from jax.experimental.pallas import tpu as pltpu
from jax.sharding import PartitionSpec as P


NT = 1024
NF = 256
GRID = 576
SPREAD = 512
DEV = 128
ROWS = 4
NS = 16
NPT = 8
SHARE = 64
VMEM = 56 * 1024 * 1024
BLOCKS = 8
PITCH = 40


def band_tables():
    phase = (np.arange(NT)[:, None] * np.arange(NF)[None, :]) % NT
    angle = phase.astype(np.float32) * np.float32(2.0 * math.pi / NT)
    cosine = np.cos(angle).T
    sine = np.sin(angle).T
    weights = np.where(np.arange(NF) == 0, 1.0, 2.0).astype(np.float32)[:, None] / np.float32(NT)
    forward = np.stack([cosine[0::2], -sine[0::2], cosine[1::2], -sine[1::2]])
    wc, ws = weights * cosine, -weights * sine
    inverse = np.stack([wc[0::2], ws[0::2], wc[1::2], ws[1::2]])
    forward = jnp.asarray(forward.reshape(ROWS * DEV, NT), jnp.bfloat16)
    inverse = jnp.asarray(inverse.reshape(ROWS * DEV, NT), jnp.bfloat16)
    return forward, inverse


def iota(shape, dim):
    return lax.broadcasted_iota(jnp.int32, shape, dim)


def dot_nt(left, right):
    return lax.dot_general(left, right, (((1,), (1,)), ((), ())), preferred_element_type=jnp.float32)


def dot_nn(left, right):
    return jnp.dot(left, right, preferred_element_type=jnp.float32)


def unpack(in_ref, rows):
    for d in range(DEV):
        rows[d * PITCH : d * PITCH + 32] = in_ref[d].astype(jnp.float32)


def order_matrix(slot_ref, mask_ref):
    f32, b16 = jnp.float32, jnp.bfloat16
    wide = NS * NS
    spread = (iota((NS, wide), 1) % NS == iota((NS, wide), 0)).astype(f32).astype(b16)
    owner = lax.shift_right_logical(slot_ref[...], 3).astype(f32).astype(b16)
    owner = dot_nn(jnp.broadcast_to(owner, (NS, NS)), spread)[0:1].astype(jnp.int32)
    taper = dot_nn(mask_ref[...].astype(f32).astype(b16), spread)
    taper = jnp.where(iota((NS, wide), 1) // NS == iota((NS, wide), 0), taper, 0.0)
    taper = jnp.sum(taper, axis=0, keepdims=True)
    r, l = iota((wide, wide), 0), iota((wide, wide), 1)
    return jnp.where((r // NS == l // NS) & (owner == r % NS), taper, 0.0).astype(b16)


def forward_kernel(
    shot_any, store_any, slot_any, mask_any, start_any, table_any, out_ref,
    shot, store, slot, mask, first, table, rows, sems,
):
    f32, b16 = jnp.float32, jnp.bfloat16
    parts = [pl.ds(0, 256), pl.ds(256, 256), pl.ds(512, 64)]
    pairs = [(slot_any, slot), (mask_any, mask), (start_any, first), (table_any, table), (shot_any, shot)]
    pairs += [(store_any.at[0, part], store.at[part]) for part in parts]
    loads = [pltpu.make_async_copy(src, dst, sems.at[n]) for n, (src, dst) in enumerate(pairs)]
    for load in loads:
        load.start()
    for load in loads[:3]:
        load.wait()
    order = order_matrix(slot, mask)
    pick = (iota((NS, 128), 1) - 64 == iota((NS, 128), 0)).astype(f32).astype(b16)
    start = first[...].astype(f32).astype(b16)
    start = dot_nn(jnp.broadcast_to(start, (NS, NS)), pick)[0:1]
    for c in range(ROWS):
        rows[pl.ds(28 + c, DEV, PITCH), :] = jnp.zeros((DEV, 128), f32)

    def put(block, value):
        for n in range(value.shape[1] // 128):
            for c in range(ROWS):
                rows[pl.ds(4 * (block + n) + c, DEV, PITCH), :] = value[c * DEV : (c + 1) * DEV, 128 * n : 128 * (n + 1)]

    loads[3].wait()
    loads[4].wait()
    spectra = dot_nt(table[...], shot[...].reshape(NS * NS, NT)).astype(b16)
    put(0, dot_nt(spectra, order))
    for h in range(2):
        loads[5 + h].wait()
        put(2 + 2 * h, dot_nt(table[...], store[256 * h : 256 * (h + 1)]))
    loads[7].wait()
    tail = jnp.concatenate([store[SPREAD:GRID], jnp.zeros((64, NT), b16)], axis=0)
    put(6, dot_nt(table[...], tail) + start)
    for d in range(DEV):
        out_ref[d] = rows[d * PITCH : d * PITCH + 32].astype(b16)


def product_kernel(in_ref, out_ref, rows, left, prod, wins):
    f32, b16 = jnp.float32, jnp.bfloat16
    unpack(in_ref, rows)

    def piece(block, c):
        return rows[pl.ds(4 * block + c, DEV, PITCH), :]

    a, b = iota((128, 1024), 0), iota((128, 1024), 1)
    tile = ((a // 16 == b // 128) & (a % 16 == (b % 128) // 8)).astype(f32).astype(b16)
    halves = []
    keep = iota((512, 1024), 0) % 8 == iota((512, 1024), 1) % 8
    fold = (iota((64, 512), 0) == iota((64, 512), 1) // 8).astype(f32).astype(b16)
    for half in range(2):
        arrived = jnp.concatenate([piece(half, c) for c in range(ROWS)], axis=0).astype(b16)
        spread = dot_nn(arrived, tile)
        spread = jnp.where(keep, spread, 0.0).astype(b16)
        halves.append(dot_nn(fold, spread))

    def product(f):
        for s in range(NS):
            part = halves[s // 8][:, (s % 8) * 128 : (s % 8 + 1) * 128]
            re = part[(2 * f) * NS : (2 * f + 1) * NS]
            im = part[(2 * f + 1) * NS : (2 * f + 2) * NS]
            left[f, s * NS : (s + 1) * NS, 0:128] = re.astype(b16)
            left[f, s * NS : (s + 1) * NS, 128:256] = (-im).astype(b16)
            left[f, 256 + s * NS : 256 + (s + 1) * NS, 0:128] = im.astype(b16)
            left[f, 256 + s * NS : 256 + (s + 1) * NS, 128:256] = re.astype(b16)
        for n, blocks in ((0, 2), (2, 2), (4, 1)):
            right = jnp.concatenate(
                [
                    jnp.concatenate([piece(2 + n + m, 2 * f + part) for m in range(blocks)], axis=1)
                    for part in range(2)
                ],
                axis=0,
            ).astype(b16)
            prod[f * 512 : (f + 1) * 512, 128 * n : 128 * (n + blocks)] = dot_nn(left[f], right)

    first = rows[pl.ds(24, NS, PITCH * NPT), :][:, 64:80]
    lane = iota((NS, 128), 1)
    low = lane < 64

    def cut(f, pair):
        begin = [
            jnp.broadcast_to(first[:, 2 * pair + e : 2 * pair + e + 1], (NS, 128)).astype(jnp.int32) for e in range(2)
        ]
        at = [lane + begin[0], lane + begin[1] + 64]
        index = [x & 127 for x in at]
        here = [at[0] < 128, (lane >= 64) | (at[1] < 128)]
        for c in (2 * f, 2 * f + 1):
            base = c * 256 + 2 * pair * NS
            ahead = [None, None]
            for v in range(4, -1, -1):
                tiles = []
                for e in range(2):
                    src = prod[base + e * NS : base + (e + 1) * NS, 128 * v : 128 * (v + 1)]
                    turned = jnp.take_along_axis(src, index[e], axis=1)
                    if v < 4:
                        tiles.append(jnp.where(here[e], turned, ahead[e]))
                    ahead[e] = turned
                if v < 4:
                    slot = c * 8 + pair
                    wins[pl.ds(2 * v * NS * PITCH + slot, NS, PITCH), :] = jnp.where(low, tiles[0], tiles[1])
                    wins[pl.ds((2 * v + 1) * NS * PITCH + slot, NS, PITCH), :] = jnp.where(low, tiles[1], tiles[0])

    product(0)
    for pair in range(4):
        cut(0, pair)
    product(1)
    for pair in range(4, 8):
        cut(0, pair)
    for pair in range(8):
        cut(1, pair)
    for d in range(DEV):
        at = (d % NPT * NS + d // NPT) * PITCH
        out_ref[d] = wins[at : at + 32].astype(b16)


def inverse_kernel(in_ref, table_ref, out_any, rows, result, sems):
    swap = lax.axis_index("pt") % 2
    unpack(in_ref, rows)
    pairs = NS // 2 // BLOCKS
    copies = []
    for block in range(BLOCKS):
        left = jnp.concatenate(
            [
                jnp.concatenate([rows[pl.ds(c * 8 + pair, DEV, PITCH), :].T for c in range(ROWS)], axis=1)
                for pair in range(block * pairs, (block + 1) * pairs)
            ],
            axis=0,
        ).astype(jnp.bfloat16)
        shots = pl.ds(2 * pairs * block, 2 * pairs)
        traces = dot_nn(left, table_ref[...])
        for pair in range(pairs):
            for e in range(2):
                place = 2 * (block * pairs + pair) + (swap if e == 0 else 1 - swap)
                result[place] = traces[(2 * pair + e) * SHARE : (2 * pair + e + 1) * SHARE]
        copies.append(pltpu.make_async_copy(result.at[shots], out_any.at[shots], sems.at[block]))
        copies[-1].start()
    for copy in copies:
        copy.wait()


PARAMS = pltpu.CompilerParams(vmem_limit_bytes=VMEM)


def run_forward(shot_data, point_store, point_slot, taper_mask, recv_start):
    return pl.pallas_call(
        forward_kernel,
        out_shape=pltpu.VMEM((DEV, 32, 128), jnp.bfloat16), out_specs=pl.BlockSpec(memory_space=pltpu.VMEM),
        in_specs=[pl.BlockSpec(memory_space=pl.ANY)] * 6,
        scratch_shapes=[
            pltpu.VMEM((NS, NS, NT), jnp.bfloat16),
            pltpu.VMEM((GRID, NT), jnp.bfloat16),
            pltpu.VMEM((1, NS), jnp.int32),
            pltpu.VMEM((NS, NS), jnp.int32),
            pltpu.VMEM((1, NS), jnp.int32),
            pltpu.VMEM((ROWS * DEV, NT), jnp.bfloat16),
            pltpu.VMEM((DEV * PITCH, 128), jnp.float32),
            pltpu.SemaphoreType.DMA((8,)),
        ],
        compiler_params=PARAMS,
        name="forward",
    )(shot_data, point_store, point_slot.reshape(1, NS), taper_mask, recv_start.reshape(1, NS), band_tables()[0])


def run_product(got):
    return pl.pallas_call(
        product_kernel,
        out_shape=pltpu.VMEM((DEV, 32, 128), jnp.bfloat16), out_specs=pl.BlockSpec(memory_space=pltpu.VMEM),
        scratch_shapes=[
            pltpu.VMEM((DEV * PITCH, 128), jnp.float32),
            pltpu.VMEM((2, 512, 256), jnp.bfloat16),
            pltpu.VMEM((1024, 640), jnp.float32),
            pltpu.VMEM((DEV * PITCH, 128), jnp.float32),
        ],
        compiler_params=PARAMS,
        name="product",
        in_specs=[pl.BlockSpec(memory_space=pltpu.VMEM)],
    )(pltpu.with_memory_space_constraint(got, pltpu.VMEM))


def run_inverse(back):
    vmem = lambda x: pltpu.with_memory_space_constraint(x, pltpu.VMEM)
    return pl.pallas_call(
        inverse_kernel,
        in_specs=[pl.BlockSpec(memory_space=pltpu.VMEM)] * 2,
        out_specs=pl.BlockSpec(memory_space=pl.ANY),
        out_shape=jax.ShapeDtypeStruct((NS, SHARE, NT), jnp.float32),
        scratch_shapes=[
            pltpu.VMEM((DEV * PITCH, 128), jnp.float32),
            pltpu.VMEM((NS, SHARE, NT), jnp.float32),
            pltpu.SemaphoreType.DMA((BLOCKS,)),
        ],
        compiler_params=PARAMS,
        name="inverse",
    )(vmem(back), vmem(band_tables()[1]))


def per_device(shot_data, point_store, point_slot, taper_mask, recv_start):
    sent = run_forward(shot_data, point_store, point_slot, taper_mask, recv_start)
    got = lax.all_to_all(sent, ("shot", "pt"), 0, 0, tiled=True)
    back = lax.all_to_all(run_product(got), ("shot", "pt"), 0, 0, tiled=True)
    return run_inverse(back)


def solution(mesh):
    placed = (
        P("shot", "pt", None),
        P(("shot", "pt"), None, None),
        P("pt"),
        P("shot", "pt"),
        P("shot"),
    )
    return jax.shard_map(
        per_device, mesh=mesh, in_specs=placed, out_specs=P("shot", "pt", None), check_vma=False
    )
```

profile of v0, /device:TPU:1, one launch (start us, length us, event | category | flops | bytes accessed | tf_op | source)
XLA Modules:
  0.0 64.2 jit_solution(12791639284709586201)
XLA Ops:
  0.0 0.0 copy-start
  0.0 4.6 %forward.1 = bf16[128,32,128]{2,1,0:T(8,128)(2,1)S(1)} custom-call(bf16[16,16,1024]{2,1,0:T(8,128)(2,1)} %shot_any.1, bf16[1,576,1024]{2,1,0:T(8,128)(2,1)} %store_any.1, s32[1,16]{1,0:T(1,128)} %bitcast.2, s32[16,16]{1,0:T(8,128)} %mask_any.1, s32[1,16]{1,0:T(1,128)} %bitcast.3, bf16[512,1024]{1,0:T(8,128)(2,1)} %constant.4.clone.table_any), custom_call_target="tpu_custom_call" | custom-call | tf_op jit(solution)/shard_map/forward/pallas_call | solution.py:216
  4.6 30.7 %all_to_all.10.in_ref = bf16[128,32,128]{2,1,0:T(8,128)(2,1)S(1)} all-to-all(bf16[128,32,128]{2,1,0:T(8,128)(2,1)S(1)} %forward.1), channel_id=1, replica_groups=mesh['shot'=16,'pt'=8] {'shot','pt'}, dimensions={0} | all-to-all | bytes 2097152 | tf_op jit(solution)/shard_map/all_to_all | solution.py:270
  35.3 2.9 %product.1 = bf16[128,32,128]{2,1,0:T(8,128)(2,1)S(1)} custom-call(bf16[128,32,128]{2,1,0:T(8,128)(2,1)S(1)} %all_to_all.10.in_ref), custom_call_target="tpu_custom_call" | custom-call | tf_op jit(solution)/shard_map/product/pallas_call | solution.py:236
  38.2 23.4 %all_to_all.11.in_ref = bf16[128,32,128]{2,1,0:T(8,128)(2,1)S(1)} all-to-all(bf16[128,32,128]{2,1,0:T(8,128)(2,1)S(1)} %product.1), channel_id=1, replica_groups=mesh['shot'=16,'pt'=8] {'shot','pt'}, dimensions={0} | all-to-all | bytes 2097152 | tf_op jit(solution)/shard_map/all_to_all | solution.py:271
  61.6 0.0 copy-done
  61.6 2.6 %inverse.1 = f32[16,64,1024]{2,1,0:T(8,128)} custom-call(bf16[128,32,128]{2,1,0:T(8,128)(2,1)S(1)} %all_to_all.11.in_ref, bf16[512,1024]{1,0:T(8,128)(2,1)S(1)} %copy-done), custom_call_target="tpu_custom_call" | custom-call | tf_op jit(solution)/shard_map/inverse/pallas_call | solution.py:253
Async XLA Ops:
  0.0 61.6 %copy-start = (bf16[512,1024]{1,0:T(8,128)(2,1)S(1)}, bf16[512,1024]{1,0:T(8,128)(2,1)}, u32[]{:S(2)}) copy-start(bf16[512,1024]{1,0:T(8,128)(2,1)} %constant.5.clone.table_ref) | copy-start | bytes 3145732
where the time goes:
time: 64.3 us; the launch traced here: 64.2 us
  blocking collectives  54 us (84%)
  Pallas kernels  10.1 us (16%)
    all_to_all x1, blocking collectives, per_device(): got = lax.all_to_all(sent, ('shot', 'pt'), 0, 0, tiled=True)  30.7 us
    all_to_all x1, blocking collectives, per_device(): back = lax.all_to_all(run_product(got), ('shot', 'pt'), 0, 0, tiled=True)  23.4 us
    pallas_call x1, Pallas kernels, run_forward(): pl.pallas_call(forward_kernel, out_shape=pltpu.VMEM((DEV, 32, 128), jnp.b...  4.61 us
    pallas_call x1, Pallas kernels, run_product(): pl.pallas_call(product_kernel, out_shape=pltpu.VMEM((DEV, 32, 128), jnp.b...  2.89 us
    pallas_call x1, Pallas kernels, run_inverse(): pl.pallas_call(inverse_kernel, in_specs=[pl.BlockSpec(memory_space=pltpu....  2.6 us

commit v1 on v0

--- a/solution.py
+++ b/solution.py
@@ -30,7 +30,7 @@
     cosine = np.cos(angle).T
     sine = np.sin(angle).T
     weights = np.where(np.arange(NF) == 0, 1.0, 2.0).astype(np.float32)[:, None] / np.float32(NT)
-    forward = np.stack([cosine[0::2], -sine[0::2], cosine[1::2], -sine[1::2]])
+    forward = np.stack([cosine, -sine], axis=1)
     wc, ws = weights * cosine, -weights * sine
     inverse = np.stack([wc[0::2], ws[0::2], wc[1::2], ws[1::2]])
     forward = jnp.asarray(forward.reshape(ROWS * DEV, NT), jnp.bfloat16)
@@ -70,7 +70,7 @@
 
 def forward_kernel(
     shot_any, store_any, slot_any, mask_any, start_any, table_any, out_ref,
-    shot, store, slot, mask, first, table, rows, sems,
+    shot, store, slot, mask, first, table, sems,
 ):
     f32, b16 = jnp.float32, jnp.bfloat16
     parts = [pl.ds(0, 256), pl.ds(256, 256), pl.ds(512, 64)]
@@ -85,13 +85,9 @@
     pick = (iota((NS, 128), 1) - 64 == iota((NS, 128), 0)).astype(f32).astype(b16)
     start = first[...].astype(f32).astype(b16)
     start = dot_nn(jnp.broadcast_to(start, (NS, NS)), pick)[0:1]
-    for c in range(ROWS):
-        rows[pl.ds(28 + c, DEV, PITCH), :] = jnp.zeros((DEV, 128), f32)
-
     def put(block, value):
         for n in range(value.shape[1] // 128):
-            for c in range(ROWS):
-                rows[pl.ds(4 * (block + n) + c, DEV, PITCH), :] = value[c * DEV : (c + 1) * DEV, 128 * n : 128 * (n + 1)]
+            out_ref[:, block + n] = value[:, 128 * n : 128 * (n + 1)].reshape(DEV, ROWS, 128).astype(b16)
 
     loads[3].wait()
     loads[4].wait()
@@ -103,16 +99,15 @@
     loads[7].wait()
     tail = jnp.concatenate([store[SPREAD:GRID], jnp.zeros((64, NT), b16)], axis=0)
     put(6, dot_nt(table[...], tail) + start)
-    for d in range(DEV):
-        out_ref[d] = rows[d * PITCH : d * PITCH + 32].astype(b16)
 
 
 def product_kernel(in_ref, out_ref, rows, left, prod, wins):
     f32, b16 = jnp.float32, jnp.bfloat16
-    unpack(in_ref, rows)
+    for block in range(7):
+        rows[block] = in_ref[:, block].astype(f32).reshape(DEV * ROWS, 128)
 
     def piece(block, c):
-        return rows[pl.ds(4 * block + c, DEV, PITCH), :]
+        return rows[block, pl.ds(c, DEV, ROWS), :]
 
     a, b = iota((128, 1024), 0), iota((128, 1024), 1)
     tile = ((a // 16 == b // 128) & (a % 16 == (b % 128) // 8)).astype(f32).astype(b16)
@@ -144,7 +139,7 @@
             ).astype(b16)
             prod[f * 512 : (f + 1) * 512, 128 * n : 128 * (n + blocks)] = dot_nn(left[f], right)
 
-    first = rows[pl.ds(24, NS, PITCH * NPT), :][:, 64:80]
+    first = rows[6, pl.ds(0, NS, ROWS * NPT), :][:, 64:80]
     lane = iota((NS, 128), 1)
     low = lane < 64
 
@@ -215,7 +210,7 @@
 def run_forward(shot_data, point_store, point_slot, taper_mask, recv_start):
     return pl.pallas_call(
         forward_kernel,
-        out_shape=pltpu.VMEM((DEV, 32, 128), jnp.bfloat16), out_specs=pl.BlockSpec(memory_space=pltpu.VMEM),
+        out_shape=pltpu.VMEM((DEV, 7, ROWS, 128), jnp.bfloat16), out_specs=pl.BlockSpec(memory_space=pltpu.VMEM),
         in_specs=[pl.BlockSpec(memory_space=pl.ANY)] * 6,
         scratch_shapes=[
             pltpu.VMEM((NS, NS, NT), jnp.bfloat16),
@@ -224,7 +219,6 @@
             pltpu.VMEM((NS, NS), jnp.int32),
             pltpu.VMEM((1, NS), jnp.int32),
             pltpu.VMEM((ROWS * DEV, NT), jnp.bfloat16),
-            pltpu.VMEM((DEV * PITCH, 128), jnp.float32),
             pltpu.SemaphoreType.DMA((8,)),
         ],
         compiler_params=PARAMS,
@@ -237,7 +231,7 @@
         product_kernel,
         out_shape=pltpu.VMEM((DEV, 32, 128), jnp.bfloat16), out_specs=pl.BlockSpec(memory_space=pltpu.VMEM),
         scratch_shapes=[
-            pltpu.VMEM((DEV * PITCH, 128), jnp.float32),
+            pltpu.VMEM((7, DEV * ROWS, 128), jnp.float32),
             pltpu.VMEM((2, 512, 256), jnp.bfloat16),
             pltpu.VMEM((1024, 640), jnp.float32),
             pltpu.VMEM((DEV * PITCH, 128), jnp.float32),

time: 64.3 us -> 62.8 us (0.977)
  blocking collectives: 54 us -> 52.6 us
    all_to_all x1, blocking collectives: 30.7 us -> 29.3 us  [per_device(): got = lax.all_to_all(sent, ('shot', 'pt'), 0, 0, tiled=True)]
where the time goes in v1:
time: 62.8 us; the launch traced here: 62.6 us
  blocking collectives  52.6 us (84%)
  Pallas kernels  9.99 us (16%)
    all_to_all x1, blocking collectives, per_device(): got = lax.all_to_all(sent, ('shot', 'pt'), 0, 0, tiled=True)  29.3 us
    all_to_all x1, blocking collectives, per_device(): back = lax.all_to_all(run_product(got), ('shot', 'pt'), 0, 0, tiled=True)  23.4 us
    pallas_call x1, Pallas kernels, run_forward(): pl.pallas_call(forward_kernel, out_shape=pltpu.VMEM((DEV, 7, ROWS, 128),...  4.54 us
    pallas_call x1, Pallas kernels, run_product(): pl.pallas_call(product_kernel, out_shape=pltpu.VMEM((DEV, 32, 128), jnp.b...  2.85 us
    pallas_call x1, Pallas kernels, run_inverse(): pl.pallas_call(inverse_kernel, in_specs=[pl.BlockSpec(memory_space=pltpu....  2.6 us

profile of v1, /device:TPU:1, one launch (start us, length us, event | category | flops | bytes accessed | tf_op | source)
XLA Modules:
  0.0 62.6 jit_solution(6691690064281047211)
XLA Ops:
  0.0 0.0 copy-start
  0.0 4.5 %forward.1 = bf16[128,7,4,128]{3,2,1,0:T(4,128)(2,1)S(1)} custom-call(bf16[16,16,1024]{2,1,0:T(8,128)(2,1)} %shot_any.1, bf16[1,576,1024]{2,1,0:T(8,128)(2,1)} %store_any.1, s32[1,16]{1,0:T(1,128)} %bitcast.2, s32[16,16]{1,0:T(8,128)} %mask_any.1, s32[1,16]{1,0:T(1,128)} %bitcast.3, bf16[512,1024]{1,0:T(8,128)(2,1)} %constant.4.clone.table_any), custom_call_target="tpu_custom_call" | custom-call | tf_op jit(solution)/shard_map/forward/pallas_call | solution.py:211
  4.5 29.3 %all_to_all.10.in_ref = bf16[128,7,4,128]{3,2,1,0:T(4,128)(2,1)S(1)} all-to-all(bf16[128,7,4,128]{3,2,1,0:T(4,128)(2,1)S(1)} %forward.1), channel_id=1, replica_groups=mesh['shot'=16,'pt'=8] {'shot','pt'}, dimensions={0} | all-to-all | bytes 1835008 | tf_op jit(solution)/shard_map/all_to_all | solution.py:264
  33.8 2.9 %product.1 = bf16[128,32,128]{2,1,0:T(8,128)(2,1)S(1)} custom-call(bf16[128,7,4,128]{3,2,1,0:T(4,128)(2,1)S(1)} %all_to_all.10.in_ref), custom_call_target="tpu_custom_call" | custom-call | tf_op jit(solution)/shard_map/product/pallas_call | solution.py:230
  36.7 23.4 %all_to_all.11.in_ref = bf16[128,32,128]{2,1,0:T(8,128)(2,1)S(1)} all-to-all(bf16[128,32,128]{2,1,0:T(8,128)(2,1)S(1)} %product.1), channel_id=1, replica_groups=mesh['shot'=16,'pt'=8] {'shot','pt'}, dimensions={0} | all-to-all | bytes 2097152 | tf_op jit(solution)/shard_map/all_to_all | solution.py:265
  60.0 0.0 copy-done
  60.0 2.6 %inverse.1 = f32[16,64,1024]{2,1,0:T(8,128)} custom-call(bf16[128,32,128]{2,1,0:T(8,128)(2,1)S(1)} %all_to_all.11.in_ref, bf16[512,1024]{1,0:T(8,128)(2,1)S(1)} %copy-done), custom_call_target="tpu_custom_call" | custom-call | tf_op jit(solution)/shard_map/inverse/pallas_call | solution.py:247
Async XLA Ops:
  0.0 60.0 %copy-start = (bf16[512,1024]{1,0:T(8,128)(2,1)S(1)}, bf16[512,1024]{1,0:T(8,128)(2,1)}, u32[]{:S(2)}) copy-start(bf16[512,1024]{1,0:T(8,128)(2,1)} %constant.5.clone.table_ref) | copy-start | bytes 3145732

commit v2 on v1

--- a/solution.py
+++ b/solution.py
@@ -20,7 +20,6 @@
 NPT = 8
 SHARE = 64
 VMEM = 56 * 1024 * 1024
-BLOCKS = 8
 PITCH = 40
 
 
@@ -31,8 +30,7 @@
     sine = np.sin(angle).T
     weights = np.where(np.arange(NF) == 0, 1.0, 2.0).astype(np.float32)[:, None] / np.float32(NT)
     forward = np.stack([cosine, -sine], axis=1)
-    wc, ws = weights * cosine, -weights * sine
-    inverse = np.stack([wc[0::2], ws[0::2], wc[1::2], ws[1::2]])
+    inverse = np.stack([weights * cosine, -weights * sine], axis=1)
     forward = jnp.asarray(forward.reshape(ROWS * DEV, NT), jnp.bfloat16)
     inverse = jnp.asarray(inverse.reshape(ROWS * DEV, NT), jnp.bfloat16)
     return forward, inverse
@@ -48,11 +46,6 @@
 
 def dot_nn(left, right):
     return jnp.dot(left, right, preferred_element_type=jnp.float32)
-
-
-def unpack(in_ref, rows):
-    for d in range(DEV):
-        rows[d * PITCH : d * PITCH + 32] = in_ref[d].astype(jnp.float32)
 
 
 def order_matrix(slot_ref, mask_ref):
@@ -73,12 +66,12 @@
     shot, store, slot, mask, first, table, sems,
 ):
     f32, b16 = jnp.float32, jnp.bfloat16
-    parts = [pl.ds(0, 256), pl.ds(256, 256), pl.ds(512, 64)]
     pairs = [(slot_any, slot), (mask_any, mask), (start_any, first), (table_any, table), (shot_any, shot)]
-    pairs += [(store_any.at[0, part], store.at[part]) for part in parts]
+    pairs += [(store_any.at[0], store.at[pl.ds(0, GRID)])]
     loads = [pltpu.make_async_copy(src, dst, sems.at[n]) for n, (src, dst) in enumerate(pairs)]
     for load in loads:
         load.start()
+    store[GRID:] = jnp.zeros((64, NT), b16)
     for load in loads[:3]:
         load.wait()
     order = order_matrix(slot, mask)
@@ -89,16 +82,13 @@
         for n in range(value.shape[1] // 128):
             out_ref[:, block + n] = value[:, 128 * n : 128 * (n + 1)].reshape(DEV, ROWS, 128).astype(b16)
 
-    loads[3].wait()
-    loads[4].wait()
+    for load in loads[3:]:
+        load.wait()
     spectra = dot_nt(table[...], shot[...].reshape(NS * NS, NT)).astype(b16)
+    gathers = dot_nt(table[...], store[...])
+    put(2, gathers[:, 0:SPREAD])
+    put(6, gathers[:, SPREAD:] + start)
     put(0, dot_nt(spectra, order))
-    for h in range(2):
-        loads[5 + h].wait()
-        put(2 + 2 * h, dot_nt(table[...], store[256 * h : 256 * (h + 1)]))
-    loads[7].wait()
-    tail = jnp.concatenate([store[SPREAD:GRID], jnp.zeros((64, NT), b16)], axis=0)
-    put(6, dot_nt(table[...], tail) + start)
 
 
 def product_kernel(in_ref, out_ref, rows, left, prod, wins):
@@ -111,24 +101,21 @@
 
     a, b = iota((128, 1024), 0), iota((128, 1024), 1)
     tile = ((a // 16 == b // 128) & (a % 16 == (b % 128) // 8)).astype(f32).astype(b16)
-    halves = []
-    keep = iota((512, 1024), 0) % 8 == iota((512, 1024), 1) % 8
-    fold = (iota((64, 512), 0) == iota((64, 512), 1) // 8).astype(f32).astype(b16)
-    for half in range(2):
-        arrived = jnp.concatenate([piece(half, c) for c in range(ROWS)], axis=0).astype(b16)
-        spread = dot_nn(arrived, tile)
-        spread = jnp.where(keep, spread, 0.0).astype(b16)
-        halves.append(dot_nn(fold, spread))
+    keep = iota((256, 1024), 0) % 8 == iota((256, 1024), 1) % 8
+    fold = (iota((32, 256), 0) == iota((32, 256), 1) // 8).astype(f32).astype(b16)
 
     def product(f):
-        for s in range(NS):
-            part = halves[s // 8][:, (s % 8) * 128 : (s % 8 + 1) * 128]
-            re = part[(2 * f) * NS : (2 * f + 1) * NS]
-            im = part[(2 * f + 1) * NS : (2 * f + 2) * NS]
-            left[f, s * NS : (s + 1) * NS, 0:128] = re.astype(b16)
-            left[f, s * NS : (s + 1) * NS, 128:256] = (-im).astype(b16)
-            left[f, 256 + s * NS : 256 + (s + 1) * NS, 0:128] = im.astype(b16)
-            left[f, 256 + s * NS : 256 + (s + 1) * NS, 128:256] = re.astype(b16)
+        for half in range(2):
+            arrived = jnp.concatenate([piece(half, c) for c in (2 * f, 2 * f + 1)], axis=0).astype(b16)
+            spread = jnp.where(keep, dot_nn(arrived, tile), 0.0).astype(b16)
+            folded = dot_nn(fold, spread)
+            for n in range(8):
+                re, im = folded[0:NS, n * 128 : (n + 1) * 128], folded[NS:, n * 128 : (n + 1) * 128]
+                top = (half * 8 + n) * NS
+                left[f, top : top + NS, 0:128] = re.astype(b16)
+                left[f, top : top + NS, 128:256] = (-im).astype(b16)
+                left[f, 256 + top : 256 + top + NS, 0:128] = im.astype(b16)
+                left[f, 256 + top : 256 + top + NS, 128:256] = re.astype(b16)
         for n, blocks in ((0, 2), (2, 2), (4, 1)):
             right = jnp.concatenate(
                 [
@@ -162,43 +149,31 @@
                         tiles.append(jnp.where(here[e], turned, ahead[e]))
                     ahead[e] = turned
                 if v < 4:
-                    slot = c * 8 + pair
+                    slot = pair * ROWS + c
                     wins[pl.ds(2 * v * NS * PITCH + slot, NS, PITCH), :] = jnp.where(low, tiles[0], tiles[1])
                     wins[pl.ds((2 * v + 1) * NS * PITCH + slot, NS, PITCH), :] = jnp.where(low, tiles[1], tiles[0])
 
     product(0)
-    for pair in range(4):
-        cut(0, pair)
     product(1)
-    for pair in range(4, 8):
+    for pair in range(8):
         cut(0, pair)
     for pair in range(8):
         cut(1, pair)
     for d in range(DEV):
         at = (d % NPT * NS + d // NPT) * PITCH
-        out_ref[d] = wins[at : at + 32].astype(b16)
-
-
-def inverse_kernel(in_ref, table_ref, out_any, rows, result, sems):
+        out_ref[d] = wins[at : at + 32].reshape(NS // 2, ROWS, 128).astype(b16)
+
+
+def inverse_kernel(in_ref, table_ref, out_any, result, sems):
     swap = lax.axis_index("pt") % 2
-    unpack(in_ref, rows)
-    pairs = NS // 2 // BLOCKS
     copies = []
-    for block in range(BLOCKS):
-        left = jnp.concatenate(
-            [
-                jnp.concatenate([rows[pl.ds(c * 8 + pair, DEV, PITCH), :].T for c in range(ROWS)], axis=1)
-                for pair in range(block * pairs, (block + 1) * pairs)
-            ],
-            axis=0,
-        ).astype(jnp.bfloat16)
-        shots = pl.ds(2 * pairs * block, 2 * pairs)
+    for pair in range(NS // 2):
+        left = in_ref[:, pair].reshape(DEV * ROWS, 128).T
         traces = dot_nn(left, table_ref[...])
-        for pair in range(pairs):
-            for e in range(2):
-                place = 2 * (block * pairs + pair) + (swap if e == 0 else 1 - swap)
-                result[place] = traces[(2 * pair + e) * SHARE : (2 * pair + e + 1) * SHARE]
-        copies.append(pltpu.make_async_copy(result.at[shots], out_any.at[shots], sems.at[block]))
+        for e in range(2):
+            result[2 * pair + (swap if e == 0 else 1 - swap)] = traces[e * SHARE : (e + 1) * SHARE]
+        shots = pl.ds(2 * pair, 2)
+        copies.append(pltpu.make_async_copy(result.at[shots], out_any.at[shots], sems.at[pair]))
         copies[-1].start()
     for copy in copies:
         copy.wait()
@@ -214,12 +189,12 @@
         in_specs=[pl.BlockSpec(memory_space=pl.ANY)] * 6,
         scratch_shapes=[
             pltpu.VMEM((NS, NS, NT), jnp.bfloat16),
-            pltpu.VMEM((GRID, NT), jnp.bfloat16),
+            pltpu.VMEM((GRID + 64, NT), jnp.bfloat16),
             pltpu.VMEM((1, NS), jnp.int32),
             pltpu.VMEM((NS, NS), jnp.int32),
             pltpu.VMEM((1, NS), jnp.int32),
             pltpu.VMEM((ROWS * DEV, NT), jnp.bfloat16),
-            pltpu.SemaphoreType.DMA((8,)),
+            pltpu.SemaphoreType.DMA((6,)),
         ],
         compiler_params=PARAMS,
         name="forward",
@@ -229,7 +204,7 @@
 def run_product(got):
     return pl.pallas_call(
         product_kernel,
-        out_shape=pltpu.VMEM((DEV, 32, 128), jnp.bfloat16), out_specs=pl.BlockSpec(memory_space=pltpu.VMEM),
+        out_shape=pltpu.VMEM((DEV, NS // 2, ROWS, 128), jnp.bfloat16), out_specs=pl.BlockSpec(memory_space=pltpu.VMEM),
         scratch_shapes=[
             pltpu.VMEM((7, DEV * ROWS, 128), jnp.float32),
             pltpu.VMEM((2, 512, 256), jnp.bfloat16),
@@ -250,9 +225,8 @@
         out_specs=pl.BlockSpec(memory_space=pl.ANY),
         out_shape=jax.ShapeDtypeStruct((NS, SHARE, NT), jnp.float32),
         scratch_shapes=[
-            pltpu.VMEM((DEV * PITCH, 128), jnp.float32),
             pltpu.VMEM((NS, SHARE, NT), jnp.float32),
-            pltpu.SemaphoreType.DMA((BLOCKS,)),
+            pltpu.SemaphoreType.DMA((NS // 2,)),
         ],
         compiler_params=PARAMS,
         name="inverse",

time: 62.8 us -> 61.2 us (0.975)
  Pallas kernels: 9.99 us -> 8.45 us
    pallas_call x1, Pallas kernels: 4.54 us -> 3.31 us  [run_forward(): pl.pallas_call(forward_kernel, out_shape=pltpu.VMEM((DEV, 7, ROWS, 128),...]
where the time goes in v2:
time: 61.2 us; the launch traced here: 61.1 us
  blocking collectives  52.6 us (86%)
  Pallas kernels  8.45 us (14%)
    all_to_all x1, blocking collectives, per_device(): got = lax.all_to_all(sent, ('shot', 'pt'), 0, 0, tiled=True)  29.3 us
    all_to_all x1, blocking collectives, per_device(): back = lax.all_to_all(run_product(got), ('shot', 'pt'), 0, 0, tiled=True)  23.4 us
    pallas_call x1, Pallas kernels, run_forward(): pl.pallas_call(forward_kernel, out_shape=pltpu.VMEM((DEV, 7, ROWS, 128),...  3.31 us
    pallas_call x1, Pallas kernels, run_product(): pl.pallas_call(product_kernel, out_shape=pltpu.VMEM((DEV, NS // 2, ROWS,...  2.72 us
    pallas_call x1, Pallas kernels, run_inverse(): pl.pallas_call(inverse_kernel, in_specs=[pl.BlockSpec(memory_space=pltpu....  2.42 us

profile of v2, /device:TPU:1, one launch (start us, length us, event | category | flops | bytes accessed | tf_op | source)
XLA Modules:
  0.0 61.1 jit_solution(2056277879798855362)
XLA Ops:
  0.0 0.0 copy-start
  0.0 3.3 %forward.1 = bf16[128,7,4,128]{3,2,1,0:T(4,128)(2,1)S(1)} custom-call(bf16[16,16,1024]{2,1,0:T(8,128)(2,1)} %shot_any.1, bf16[1,576,1024]{2,1,0:T(8,128)(2,1)} %store_any.1, s32[1,16]{1,0:T(1,128)} %bitcast.2, s32[16,16]{1,0:T(8,128)} %mask_any.1, s32[1,16]{1,0:T(1,128)} %bitcast.3, bf16[512,1024]{1,0:T(8,128)(2,1)} %constant.4.clone.table_any), custom_call_target="tpu_custom_call" | custom-call | tf_op jit(solution)/shard_map/forward/pallas_call | solution.py:186
  3.3 29.3 %all_to_all.10.in_ref = bf16[128,7,4,128]{3,2,1,0:T(4,128)(2,1)S(1)} all-to-all(bf16[128,7,4,128]{3,2,1,0:T(4,128)(2,1)S(1)} %forward.1), channel_id=1, replica_groups=mesh['shot'=16,'pt'=8] {'shot','pt'}, dimensions={0} | all-to-all | bytes 1835008 | tf_op jit(solution)/shard_map/all_to_all | solution.py:238
  32.6 2.7 %product.1 = bf16[128,8,4,128]{3,2,1,0:T(4,128)(2,1)S(1)} custom-call(bf16[128,7,4,128]{3,2,1,0:T(4,128)(2,1)S(1)} %all_to_all.10.in_ref), custom_call_target="tpu_custom_call" | custom-call | tf_op jit(solution)/shard_map/product/pallas_call | solution.py:205
  35.3 23.4 %all_to_all.11.in_ref = bf16[128,8,4,128]{3,2,1,0:T(4,128)(2,1)S(1)} all-to-all(bf16[128,8,4,128]{3,2,1,0:T(4,128)(2,1)S(1)} %product.1), channel_id=1, replica_groups=mesh['shot'=16,'pt'=8] {'shot','pt'}, dimensions={0} | all-to-all | bytes 2097152 | tf_op jit(solution)/shard_map/all_to_all | solution.py:239
  58.7 0.0 copy-done
  58.7 2.4 %inverse.1 = f32[16,64,1024]{2,1,0:T(8,128)} custom-call(bf16[128,8,4,128]{3,2,1,0:T(4,128)(2,1)S(1)} %all_to_all.11.in_ref, bf16[512,1024]{1,0:T(8,128)(2,1)S(1)} %copy-done), custom_call_target="tpu_custom_call" | custom-call | tf_op jit(solution)/shard_map/inverse/pallas_call | solution.py:222
Async XLA Ops:
  0.0 58.7 %copy-start = (bf16[512,1024]{1,0:T(8,128)(2,1)S(1)}, bf16[512,1024]{1,0:T(8,128)(2,1)}, u32[]{:S(2)}) copy-start(bf16[512,1024]{1,0:T(8,128)(2,1)} %constant.5.clone.table_ref) | copy-start | bytes 3145732

commit v3 on v2

--- a/solution.py
+++ b/solution.py
@@ -19,6 +19,7 @@
 NS = 16
 NPT = 8
 SHARE = 64
+SHOTROWS = NS * NS
 VMEM = 56 * 1024 * 1024
 PITCH = 40
 
@@ -31,7 +32,7 @@
     weights = np.where(np.arange(NF) == 0, 1.0, 2.0).astype(np.float32)[:, None] / np.float32(NT)
     forward = np.stack([cosine, -sine], axis=1)
     inverse = np.stack([weights * cosine, -weights * sine], axis=1)
-    forward = jnp.asarray(forward.reshape(ROWS * DEV, NT), jnp.bfloat16)
+    forward = jnp.asarray(forward.reshape(ROWS * DEV, NT).T, jnp.bfloat16)
     inverse = jnp.asarray(inverse.reshape(ROWS * DEV, NT), jnp.bfloat16)
     return forward, inverse
 
@@ -66,67 +67,78 @@
     shot, store, slot, mask, first, table, sems,
 ):
     f32, b16 = jnp.float32, jnp.bfloat16
-    pairs = [(slot_any, slot), (mask_any, mask), (start_any, first), (table_any, table), (shot_any, shot)]
-    pairs += [(store_any.at[0], store.at[pl.ds(0, GRID)])]
+    pairs = [(slot_any, slot), (mask_any, mask), (start_any, first), (table_any, table)]
+    pairs += [(shot_any, shot), (store_any.at[0], store)]
     loads = [pltpu.make_async_copy(src, dst, sems.at[n]) for n, (src, dst) in enumerate(pairs)]
     for load in loads:
         load.start()
-    store[GRID:] = jnp.zeros((64, NT), b16)
     for load in loads[:3]:
         load.wait()
     order = order_matrix(slot, mask)
-    pick = (iota((NS, 128), 1) - 64 == iota((NS, 128), 0)).astype(f32).astype(b16)
-    start = first[...].astype(f32).astype(b16)
-    start = dot_nn(jnp.broadcast_to(start, (NS, NS)), pick)[0:1]
-    def put(block, value):
-        for n in range(value.shape[1] // 128):
-            out_ref[:, block + n] = value[:, 128 * n : 128 * (n + 1)].reshape(DEV, ROWS, 128).astype(b16)
-
+    start = jnp.broadcast_to(first[...].astype(f32).astype(b16), (NS, NS))
+    start = jnp.where(iota((NS, NS), 0) == iota((NS, NS), 1), start, 0).astype(b16)
+    start = dot_nn(start, jnp.ones((NS, ROWS * DEV), b16)).astype(b16)
+    start = jnp.concatenate([start, jnp.zeros((64 - NS, ROWS * DEV), b16)], axis=0)
     for load in loads[3:]:
         load.wait()
-    spectra = dot_nt(table[...], shot[...].reshape(NS * NS, NT)).astype(b16)
-    gathers = dot_nt(table[...], store[...])
-    put(2, gathers[:, 0:SPREAD])
-    put(6, gathers[:, SPREAD:] + start)
-    put(0, dot_nt(spectra, order))
+
+    def put(block, value):
+        for n in range(value.shape[0] // 128):
+            out_ref[:, block + n] = value[128 * n : 128 * (n + 1)].T.reshape(DEV, ROWS, 128)
+
+    spectra = dot_nn(shot[...].reshape(SHOTROWS, NT), table[...]).astype(b16)
+    put(2, jnp.concatenate([dot_nn(store[...], table[...]).astype(b16), start], axis=0))
+    put(0, dot_nn(order, spectra).astype(b16))
 
 
 def product_kernel(in_ref, out_ref, rows, left, prod, wins):
     f32, b16 = jnp.float32, jnp.bfloat16
     for block in range(7):
-        rows[block] = in_ref[:, block].astype(f32).reshape(DEV * ROWS, 128)
-
-    def piece(block, c):
-        return rows[block, pl.ds(c, DEV, ROWS), :]
-
-    a, b = iota((128, 1024), 0), iota((128, 1024), 1)
-    tile = ((a // 16 == b // 128) & (a % 16 == (b % 128) // 8)).astype(f32).astype(b16)
-    keep = iota((256, 1024), 0) % 8 == iota((256, 1024), 1) % 8
-    fold = (iota((32, 256), 0) == iota((32, 256), 1) // 8).astype(f32).astype(b16)
+        for s in range(NS):
+            part = in_ref[s * NPT : (s + 1) * NPT, block].astype(f32)
+            rows[block, s * PITCH : s * PITCH + NPT * ROWS] = part.reshape(NPT * ROWS, 128)
+
+    def piece(block, c, p):
+        return rows[block, pl.ds(p * ROWS + c, NS, PITCH), :]
+
+    arrived = jnp.concatenate(
+        [piece(half, c, p) for p in range(NPT) for half in range(2) for c in range(ROWS)], axis=0
+    ).astype(b16)
+    place = (iota((NS, 128), 0) == iota((NS, 128), 1) % NS).astype(f32).astype(b16)
+    zero = jnp.zeros((NS, 128), b16)
+    own = (iota((8, 256), 1) % 128 // NS)[None]
+    spectra = []
+    for n in range(4):
+        tile = [[place if s == 2 * n + m else zero for s in range(8)] for m in range(2)]
+        tile = jnp.concatenate([jnp.concatenate(rows_of, axis=0) for rows_of in tile], axis=1)
+        spread = dot_nn(arrived, tile).reshape(NPT, 16, 8, 256)
+        chosen = spread[0]
+        for p in range(1, NPT):
+            chosen = jnp.where(own == p, spread[p], chosen)
+        spectra.append(chosen.reshape(128, 256))
 
     def product(f):
-        for half in range(2):
-            arrived = jnp.concatenate([piece(half, c) for c in (2 * f, 2 * f + 1)], axis=0).astype(b16)
-            spread = jnp.where(keep, dot_nn(arrived, tile), 0.0).astype(b16)
-            folded = dot_nn(fold, spread)
-            for n in range(8):
-                re, im = folded[0:NS, n * 128 : (n + 1) * 128], folded[NS:, n * 128 : (n + 1) * 128]
-                top = (half * 8 + n) * NS
-                left[f, top : top + NS, 0:128] = re.astype(b16)
-                left[f, top : top + NS, 128:256] = (-im).astype(b16)
-                left[f, 256 + top : 256 + top + NS, 0:128] = im.astype(b16)
-                left[f, 256 + top : 256 + top + NS, 128:256] = re.astype(b16)
+        for s in range(NS):
+            top = s // 8 * 64 + 2 * f * NS
+            cols = slice(s % 2 * 128, (s % 2 + 1) * 128)
+            part = spectra[s % 8 // 2]
+            re, im = part[top : top + NS, cols], part[top + NS : top + 2 * NS, cols]
+            left[f, s * NS : (s + 1) * NS, 0:128] = re.astype(b16)
+            left[f, s * NS : (s + 1) * NS, 128:256] = (-im).astype(b16)
+            left[f, 256 + s * NS : 256 + (s + 1) * NS, 0:128] = im.astype(b16)
+            left[f, 256 + s * NS : 256 + (s + 1) * NS, 128:256] = re.astype(b16)
         for n, blocks in ((0, 2), (2, 2), (4, 1)):
             right = jnp.concatenate(
                 [
-                    jnp.concatenate([piece(2 + n + m, 2 * f + part) for m in range(blocks)], axis=1)
+                    jnp.concatenate([piece(2 + n + m, 2 * f + part, p) for m in range(blocks)], axis=1)
                     for part in range(2)
+                    for p in range(NPT)
                 ],
                 axis=0,
             ).astype(b16)
             prod[f * 512 : (f + 1) * 512, 128 * n : 128 * (n + blocks)] = dot_nn(left[f], right)
 
-    first = rows[6, pl.ds(0, NS, ROWS * NPT), :][:, 64:80]
+    first = piece(6, 0, 0)[:, 64:80]
     lane = iota((NS, 128), 1)
     low = lane < 64
 
@@ -185,15 +197,16 @@
 def run_forward(shot_data, point_store, point_slot, taper_mask, recv_start):
     return pl.pallas_call(
         forward_kernel,
-        out_shape=pltpu.VMEM((DEV, 7, ROWS, 128), jnp.bfloat16), out_specs=pl.BlockSpec(memory_space=pltpu.VMEM),
+        out_shape=pltpu.VMEM((DEV, 7, ROWS, 128), jnp.bfloat16),
+        out_specs=pl.BlockSpec(memory_space=pltpu.VMEM),
         in_specs=[pl.BlockSpec(memory_space=pl.ANY)] * 6,
         scratch_shapes=[
             pltpu.VMEM((NS, NS, NT), jnp.bfloat16),
-            pltpu.VMEM((GRID + 64, NT), jnp.bfloat16),
+            pltpu.VMEM((GRID, NT), jnp.bfloat16),
             pltpu.VMEM((1, NS), jnp.int32),
             pltpu.VMEM((NS, NS), jnp.int32),
             pltpu.VMEM((1, NS), jnp.int32),
-            pltpu.VMEM((ROWS * DEV, NT), jnp.bfloat16),
+            pltpu.VMEM((NT, ROWS * DEV), jnp.bfloat16),
             pltpu.SemaphoreType.DMA((6,)),
         ],
         compiler_params=PARAMS,
@@ -204,12 +217,13 @@
 def run_product(got):
     return pl.pallas_call(
         product_kernel,
-        out_shape=pltpu.VMEM((DEV, NS // 2, ROWS, 128), jnp.bfloat16), out_specs=pl.BlockSpec(memory_space=pltpu.VMEM),
+        out_shape=pltpu.VMEM((DEV, NS // 2, ROWS, 128), jnp.bfloat16),
+        out_specs=pl.BlockSpec(memory_space=pltpu.VMEM),
         scratch_shapes=[
-            pltpu.VMEM((7, DEV * ROWS, 128), jnp.float32),
+            pltpu.VMEM((7, (NS + 1) * PITCH, 128), jnp.float32),
             pltpu.VMEM((2, 512, 256), jnp.bfloat16),
             pltpu.VMEM((1024, 640), jnp.float32),
-            pltpu.VMEM((DEV * PITCH, 128), jnp.float32),
+            pltpu.VMEM(((DEV + 1) * PITCH, 128), jnp.float32),
         ],
         compiler_params=PARAMS,
         name="product",

time: 61.2 us -> 61 us (level)
  no operation moved by 1% of the time
where the time goes in v3:
time: 61 us; the launch traced here: 60.8 us
  blocking collectives  52.6 us (86%)
  Pallas kernels  8.17 us (13%)
    all_to_all x1, blocking collectives, per_device(): got = lax.all_to_all(sent, ('shot', 'pt'), 0, 0, tiled=True)  29.3 us
    all_to_all x1, blocking collectives, per_device(): back = lax.all_to_all(run_product(got), ('shot', 'pt'), 0, 0, tiled=True)  23.4 us
    pallas_call x1, Pallas kernels, run_forward(): pl.pallas_call(forward_kernel, out_shape=pltpu.VMEM((DEV, 7, ROWS, 128),...  3.17 us
    pallas_call x1, Pallas kernels, run_product(): pl.pallas_call(product_kernel, out_shape=pltpu.VMEM((DEV, NS // 2, ROWS,...  2.58 us
    pallas_call x1, Pallas kernels, run_inverse(): pl.pallas_call(inverse_kernel, in_specs=[pl.BlockSpec(memory_space=pltpu....  2.41 us

profile of v3, /device:TPU:1, one launch (start us, length us, event | category | flops | bytes accessed | tf_op | source)
XLA Modules:
  0.0 60.8 jit_solution(13345058107414668595)
XLA Ops:
  0.0 0.0 copy-start
  0.0 3.2 %forward.1 = bf16[128,7,4,128]{3,2,1,0:T(4,128)(2,1)S(1)} custom-call(bf16[16,16,1024]{2,1,0:T(8,128)(2,1)} %shot_any.1, bf16[1,576,1024]{2,1,0:T(8,128)(2,1)} %store_any.1, s32[1,16]{1,0:T(1,128)} %bitcast.2, s32[16,16]{1,0:T(8,128)} %mask_any.1, s32[1,16]{1,0:T(1,128)} %bitcast.3, bf16[1024,512]{1,0:T(8,128)(2,1)} %constant.4.clone.table_any), custom_call_target="tpu_custom_call" | custom-call | tf_op jit(solution)/shard_map/forward/pallas_call | solution.py:198
  3.2 29.3 %all_to_all.10.in_ref = bf16[128,7,4,128]{3,2,1,0:T(4,128)(2,1)S(1)} all-to-all(bf16[128,7,4,128]{3,2,1,0:T(4,128)(2,1)S(1)} %forward.1), channel_id=1, replica_groups=mesh['shot'=16,'pt'=8] {'shot','pt'}, dimensions={0} | all-to-all | bytes 1835008 | tf_op jit(solution)/shard_map/all_to_all | solution.py:252
  32.5 2.6 %product.1 = bf16[128,8,4,128]{3,2,1,0:T(4,128)(2,1)S(1)} custom-call(bf16[128,7,4,128]{3,2,1,0:T(4,128)(2,1)S(1)} %all_to_all.10.in_ref), custom_call_target="tpu_custom_call" | custom-call | tf_op jit(solution)/shard_map/product/pallas_call | solution.py:218
  35.0 23.4 %all_to_all.11.in_ref = bf16[128,8,4,128]{3,2,1,0:T(4,128)(2,1)S(1)} all-to-all(bf16[128,8,4,128]{3,2,1,0:T(4,128)(2,1)S(1)} %product.1), channel_id=1, replica_groups=mesh['shot'=16,'pt'=8] {'shot','pt'}, dimensions={0} | all-to-all | bytes 2097152 | tf_op jit(solution)/shard_map/all_to_all | solution.py:253
  58.4 0.0 copy-done
  58.4 2.4 %inverse.1 = f32[16,64,1024]{2,1,0:T(8,128)} custom-call(bf16[128,8,4,128]{3,2,1,0:T(4,128)(2,1)S(1)} %all_to_all.11.in_ref, bf16[512,1024]{1,0:T(8,128)(2,1)S(1)} %copy-done), custom_call_target="tpu_custom_call" | custom-call | tf_op jit(solution)/shard_map/inverse/pallas_call | solution.py:236
Async XLA Ops:
  0.0 58.4 %copy-start = (bf16[512,1024]{1,0:T(8,128)(2,1)S(1)}, bf16[512,1024]{1,0:T(8,128)(2,1)}, u32[]{:S(2)}) copy-start(bf16[512,1024]{1,0:T(8,128)(2,1)} %constant.5.clone.table_ref) | copy-start | bytes 3145732

commit v4 on v3

--- a/solution.py
+++ b/solution.py
@@ -32,7 +32,7 @@
     weights = np.where(np.arange(NF) == 0, 1.0, 2.0).astype(np.float32)[:, None] / np.float32(NT)
     forward = np.stack([cosine, -sine], axis=1)
     inverse = np.stack([weights * cosine, -weights * sine], axis=1)
-    forward = jnp.asarray(forward.reshape(ROWS * DEV, NT).T, jnp.bfloat16)
+    forward = jnp.asarray(forward.reshape(ROWS * DEV, NT).T[: NT // 2], jnp.bfloat16)
     inverse = jnp.asarray(inverse.reshape(ROWS * DEV, NT), jnp.bfloat16)
     return forward, inverse
 
@@ -67,7 +67,7 @@
     shot, store, slot, mask, first, table, sems,
 ):
     f32, b16 = jnp.float32, jnp.bfloat16
-    pairs = [(slot_any, slot), (mask_any, mask), (start_any, first), (table_any, table)]
+    pairs = [(slot_any, slot), (mask_any, mask), (start_any, first), (table_any, table.at[pl.ds(0, NT // 2)])]
     pairs += [(shot_any, shot), (store_any.at[0], store)]
     loads = [pltpu.make_async_copy(src, dst, sems.at[n]) for n, (src, dst) in enumerate(pairs)]
     for load in loads:
@@ -79,14 +79,17 @@
     start = jnp.where(iota((NS, NS), 0) == iota((NS, NS), 1), start, 0).astype(b16)
     start = dot_nn(start, jnp.ones((NS, ROWS * DEV), b16)).astype(b16)
     start = jnp.concatenate([start, jnp.zeros((64 - NS, ROWS * DEV), b16)], axis=0)
-    for load in loads[3:]:
-        load.wait()
+    loads[3].wait()
+    sign = jnp.where(iota((1, ROWS * DEV), 1) % ROWS < 2, 1.0, -1.0).astype(b16)
+    table[NT // 2 :] = table[: NT // 2] * sign
+    loads[4].wait()
+    spectra = dot_nn(shot[...].reshape(SHOTROWS, NT), table[...]).astype(b16)
+    loads[5].wait()
 
     def put(block, value):
         for n in range(value.shape[0] // 128):
             out_ref[:, block + n] = value[128 * n : 128 * (n + 1)].T.reshape(DEV, ROWS, 128)
 
-    spectra = dot_nn(shot[...].reshape(SHOTROWS, NT), table[...]).astype(b16)
     put(2, jnp.concatenate([dot_nn(store[...], table[...]).astype(b16), start], axis=0))
     put(0, dot_nn(order, spectra).astype(b16))
 

time: 61 us -> 60.6 us (level)
  no operation moved by 1% of the time
where the time goes in v4:
time: 60.6 us; the launch traced here: 60.5 us
  blocking collectives  52.6 us (87%)
  Pallas kernels  7.79 us (13%)
    all_to_all x1, blocking collectives, per_device(): got = lax.all_to_all(sent, ('shot', 'pt'), 0, 0, tiled=True)  29.3 us
    all_to_all x1, blocking collectives, per_device(): back = lax.all_to_all(run_product(got), ('shot', 'pt'), 0, 0, tiled=True)  23.4 us
    pallas_call x1, Pallas kernels, run_forward(): pl.pallas_call(forward_kernel, out_shape=pltpu.VMEM((DEV, 7, ROWS, 128),...  2.8 us
    pallas_call x1, Pallas kernels, run_product(): pl.pallas_call(product_kernel, out_shape=pltpu.VMEM((DEV, NS // 2, ROWS,...  2.58 us
    pallas_call x1, Pallas kernels, run_inverse(): pl.pallas_call(inverse_kernel, in_specs=[pl.BlockSpec(memory_space=pltpu....  2.41 us

profile of v4, /device:TPU:1, one launch (start us, length us, event | category | flops | bytes accessed | tf_op | source)
XLA Modules:
  0.0 60.5 jit_solution(10799620810735530971)
XLA Ops:
  0.0 0.0 copy-start
  0.0 2.8 %forward.1 = bf16[128,7,4,128]{3,2,1,0:T(4,128)(2,1)S(1)} custom-call(bf16[16,16,1024]{2,1,0:T(8,128)(2,1)} %shot_any.1, bf16[1,576,1024]{2,1,0:T(8,128)(2,1)} %store_any.1, s32[1,16]{1,0:T(1,128)} %bitcast.2, s32[16,16]{1,0:T(8,128)} %mask_any.1, s32[1,16]{1,0:T(1,128)} %bitcast.3, bf16[512,512]{1,0:T(8,128)(2,1)} %constant.4.clone.table_any), custom_call_target="tpu_custom_call" | custom-call | tf_op jit(solution)/shard_map/forward/pallas_call | solution.py:201
  2.8 29.3 %all_to_all.10.in_ref = bf16[128,7,4,128]{3,2,1,0:T(4,128)(2,1)S(1)} all-to-all(bf16[128,7,4,128]{3,2,1,0:T(4,128)(2,1)S(1)} %forward.1), channel_id=1, replica_groups=mesh['shot'=16,'pt'=8] {'shot','pt'}, dimensions={0} | all-to-all | bytes 1835008 | tf_op jit(solution)/shard_map/all_to_all | solution.py:255
  32.1 2.6 %product.1 = bf16[128,8,4,128]{3,2,1,0:T(4,128)(2,1)S(1)} custom-call(bf16[128,7,4,128]{3,2,1,0:T(4,128)(2,1)S(1)} %all_to_all.10.in_ref), custom_call_target="tpu_custom_call" | custom-call | tf_op jit(solution)/shard_map/product/pallas_call | solution.py:221
  34.7 23.4 %all_to_all.11.in_ref = bf16[128,8,4,128]{3,2,1,0:T(4,128)(2,1)S(1)} all-to-all(bf16[128,8,4,128]{3,2,1,0:T(4,128)(2,1)S(1)} %product.1), channel_id=1, replica_groups=mesh['shot'=16,'pt'=8] {'shot','pt'}, dimensions={0} | all-to-all | bytes 2097152 | tf_op jit(solution)/shard_map/all_to_all | solution.py:256
  58.0 0.0 copy-done
  58.0 2.4 %inverse.1 = f32[16,64,1024]{2,1,0:T(8,128)} custom-call(bf16[128,8,4,128]{3,2,1,0:T(4,128)(2,1)S(1)} %all_to_all.11.in_ref, bf16[512,1024]{1,0:T(8,128)(2,1)S(1)} %copy-done), custom_call_target="tpu_custom_call" | custom-call | tf_op jit(solution)/shard_map/inverse/pallas_call | solution.py:239
Async XLA Ops:
  0.0 58.0 %copy-start = (bf16[512,1024]{1,0:T(8,128)(2,1)S(1)}, bf16[512,1024]{1,0:T(8,128)(2,1)}, u32[]{:S(2)}) copy-start(bf16[512,1024]{1,0:T(8,128)(2,1)} %constant.5.clone.table_ref) | copy-start | bytes 3145732

commit v5 on v4

--- a/solution.py
+++ b/solution.py
@@ -80,9 +80,9 @@
     start = dot_nn(start, jnp.ones((NS, ROWS * DEV), b16)).astype(b16)
     start = jnp.concatenate([start, jnp.zeros((64 - NS, ROWS * DEV), b16)], axis=0)
     loads[3].wait()
+    loads[4].wait()
     sign = jnp.where(iota((1, ROWS * DEV), 1) % ROWS < 2, 1.0, -1.0).astype(b16)
     table[NT // 2 :] = table[: NT // 2] * sign
-    loads[4].wait()
     spectra = dot_nn(shot[...].reshape(SHOTROWS, NT), table[...]).astype(b16)
     loads[5].wait()
 

time: 60.6 us -> 60.6 us (level)
  no operation moved by 1% of the time
where the time goes in v5:
time: 60.6 us; the launch traced here: 60.5 us
  blocking collectives  52.6 us (87%)
  Pallas kernels  7.8 us (13%)
    all_to_all x1, blocking collectives, per_device(): got = lax.all_to_all(sent, ('shot', 'pt'), 0, 0, tiled=True)  29.3 us
    all_to_all x1, blocking collectives, per_device(): back = lax.all_to_all(run_product(got), ('shot', 'pt'), 0, 0, tiled=True)  23.4 us
    pallas_call x1, Pallas kernels, run_forward(): pl.pallas_call(forward_kernel, out_shape=pltpu.VMEM((DEV, 7, ROWS, 128),...  2.81 us
    pallas_call x1, Pallas kernels, run_product(): pl.pallas_call(product_kernel, out_shape=pltpu.VMEM((DEV, NS // 2, ROWS,...  2.58 us
    pallas_call x1, Pallas kernels, run_inverse(): pl.pallas_call(inverse_kernel, in_specs=[pl.BlockSpec(memory_space=pltpu....  2.41 us

profile of v5, /device:TPU:1, one launch (start us, length us, event | category | flops | bytes accessed | tf_op | source)
XLA Modules:
  0.0 60.5 jit_solution(3750503364759530209)
XLA Ops:
  0.0 0.0 copy-start
  0.0 2.8 %forward.1 = bf16[128,7,4,128]{3,2,1,0:T(4,128)(2,1)S(1)} custom-call(bf16[16,16,1024]{2,1,0:T(8,128)(2,1)} %shot_any.1, bf16[1,576,1024]{2,1,0:T(8,128)(2,1)} %store_any.1, s32[1,16]{1,0:T(1,128)} %bitcast.2, s32[16,16]{1,0:T(8,128)} %mask_any.1, s32[1,16]{1,0:T(1,128)} %bitcast.3, bf16[512,512]{1,0:T(8,128)(2,1)} %constant.4.clone.table_any), custom_call_target="tpu_custom_call" | custom-call | tf_op jit(solution)/shard_map/forward/pallas_call | solution.py:201
  2.8 29.3 %all_to_all.10.in_ref = bf16[128,7,4,128]{3,2,1,0:T(4,128)(2,1)S(1)} all-to-all(bf16[128,7,4,128]{3,2,1,0:T(4,128)(2,1)S(1)} %forward.1), channel_id=1, replica_groups=mesh['shot'=16,'pt'=8] {'shot','pt'}, dimensions={0} | all-to-all | bytes 1835008 | tf_op jit(solution)/shard_map/all_to_all | solution.py:255
  32.1 2.6 %product.1 = bf16[128,8,4,128]{3,2,1,0:T(4,128)(2,1)S(1)} custom-call(bf16[128,7,4,128]{3,2,1,0:T(4,128)(2,1)S(1)} %all_to_all.10.in_ref), custom_call_target="tpu_custom_call" | custom-call | tf_op jit(solution)/shard_map/product/pallas_call | solution.py:221
  34.7 23.4 %all_to_all.11.in_ref = bf16[128,8,4,128]{3,2,1,0:T(4,128)(2,1)S(1)} all-to-all(bf16[128,8,4,128]{3,2,1,0:T(4,128)(2,1)S(1)} %product.1), channel_id=1, replica_groups=mesh['shot'=16,'pt'=8] {'shot','pt'}, dimensions={0} | all-to-all | bytes 2097152 | tf_op jit(solution)/shard_map/all_to_all | solution.py:256
  58.0 0.0 copy-done
  58.0 2.4 %inverse.1 = f32[16,64,1024]{2,1,0:T(8,128)} custom-call(bf16[128,8,4,128]{3,2,1,0:T(4,128)(2,1)S(1)} %all_to_all.11.in_ref, bf16[512,1024]{1,0:T(8,128)(2,1)S(1)} %copy-done), custom_call_target="tpu_custom_call" | custom-call | tf_op jit(solution)/shard_map/inverse/pallas_call | solution.py:239
Async XLA Ops:
  0.0 58.0 %copy-start = (bf16[512,1024]{1,0:T(8,128)(2,1)S(1)}, bf16[512,1024]{1,0:T(8,128)(2,1)}, u32[]{:S(2)}) copy-start(bf16[512,1024]{1,0:T(8,128)(2,1)} %constant.5.clone.table_ref) | copy-start | bytes 3145732

commit v6 on v5

--- a/solution.py
+++ b/solution.py
@@ -70,8 +70,8 @@
     pairs = [(slot_any, slot), (mask_any, mask), (start_any, first), (table_any, table.at[pl.ds(0, NT // 2)])]
     pairs += [(shot_any, shot), (store_any.at[0], store)]
     loads = [pltpu.make_async_copy(src, dst, sems.at[n]) for n, (src, dst) in enumerate(pairs)]
-    for load in loads:
-        load.start()
+    for n in (3, 4, 0, 1, 2, 5):
+        loads[n].start()
     for load in loads[:3]:
         load.wait()
     order = order_matrix(slot, mask)

time: 60.6 us -> 60.6 us (level)
  no operation moved by 1% of the time
where the time goes in v6:
time: 60.6 us; the launch traced here: 60.4 us
  blocking collectives  52.6 us (87%)
  Pallas kernels  7.75 us (13%)
    all_to_all x1, blocking collectives, per_device(): got = lax.all_to_all(sent, ('shot', 'pt'), 0, 0, tiled=True)  29.3 us
    all_to_all x1, blocking collectives, per_device(): back = lax.all_to_all(run_product(got), ('shot', 'pt'), 0, 0, tiled=True)  23.4 us
    pallas_call x1, Pallas kernels, run_forward(): pl.pallas_call(forward_kernel, out_shape=pltpu.VMEM((DEV, 7, ROWS, 128),...  2.76 us
    pallas_call x1, Pallas kernels, run_product(): pl.pallas_call(product_kernel, out_shape=pltpu.VMEM((DEV, NS // 2, ROWS,...  2.58 us
    pallas_call x1, Pallas kernels, run_inverse(): pl.pallas_call(inverse_kernel, in_specs=[pl.BlockSpec(memory_space=pltpu....  2.41 us

profile of v6, /device:TPU:1, one launch (start us, length us, event | category | flops | bytes accessed | tf_op | source)
XLA Modules:
  0.0 60.4 jit_solution(15482984931786223267)
XLA Ops:
  0.0 0.0 copy-start
  0.0 2.8 %forward.1 = bf16[128,7,4,128]{3,2,1,0:T(4,128)(2,1)S(1)} custom-call(bf16[16,16,1024]{2,1,0:T(8,128)(2,1)} %shot_any.1, bf16[1,576,1024]{2,1,0:T(8,128)(2,1)} %store_any.1, s32[1,16]{1,0:T(1,128)} %bitcast.2, s32[16,16]{1,0:T(8,128)} %mask_any.1, s32[1,16]{1,0:T(1,128)} %bitcast.3, bf16[512,512]{1,0:T(8,128)(2,1)} %constant.4.clone.table_any), custom_call_target="tpu_custom_call" | custom-call | tf_op jit(solution)/shard_map/forward/pallas_call | solution.py:201
  2.8 29.3 %all_to_all.10.in_ref = bf16[128,7,4,128]{3,2,1,0:T(4,128)(2,1)S(1)} all-to-all(bf16[128,7,4,128]{3,2,1,0:T(4,128)(2,1)S(1)} %forward.1), channel_id=1, replica_groups=mesh['shot'=16,'pt'=8] {'shot','pt'}, dimensions={0} | all-to-all | bytes 1835008 | tf_op jit(solution)/shard_map/all_to_all | solution.py:255
  32.0 2.6 %product.1 = bf16[128,8,4,128]{3,2,1,0:T(4,128)(2,1)S(1)} custom-call(bf16[128,7,4,128]{3,2,1,0:T(4,128)(2,1)S(1)} %all_to_all.10.in_ref), custom_call_target="tpu_custom_call" | custom-call | tf_op jit(solution)/shard_map/product/pallas_call | solution.py:221
  34.6 23.4 %all_to_all.11.in_ref = bf16[128,8,4,128]{3,2,1,0:T(4,128)(2,1)S(1)} all-to-all(bf16[128,8,4,128]{3,2,1,0:T(4,128)(2,1)S(1)} %product.1), channel_id=1, replica_groups=mesh['shot'=16,'pt'=8] {'shot','pt'}, dimensions={0} | all-to-all | bytes 2097152 | tf_op jit(solution)/shard_map/all_to_all | solution.py:256
  58.0 0.0 copy-done
  58.0 2.4 %inverse.1 = f32[16,64,1024]{2,1,0:T(8,128)} custom-call(bf16[128,8,4,128]{3,2,1,0:T(4,128)(2,1)S(1)} %all_to_all.11.in_ref, bf16[512,1024]{1,0:T(8,128)(2,1)S(1)} %copy-done), custom_call_target="tpu_custom_call" | custom-call | tf_op jit(solution)/shard_map/inverse/pallas_call | solution.py:239
Async XLA Ops:
  0.0 58.0 %copy-start = (bf16[512,1024]{1,0:T(8,128)(2,1)S(1)}, bf16[512,1024]{1,0:T(8,128)(2,1)}, u32[]{:S(2)}) copy-start(bf16[512,1024]{1,0:T(8,128)(2,1)} %constant.5.clone.table_ref) | copy-start | bytes 3145732
